TPU v7x, 256 devices: a whole 4x4x8 slice. The times are simulated.
256 devices in a mesh: dp: 16 (over z, core), expert: 4 (over y), blk: 4 (over x).
Axes of the slice: x: 4, y: 4, z: 8, core: 2. Of those that a mesh axis runs over, the one named last changes fastest.
Arguments:
- tokens: bfloat16 [2048, 6144], P('dp', 'blk'), may hold values from -6 to 6
- expert_ids: int32 [2048, 2], P('dp'), may hold values from 0 to 7, all different within a row; in each aligned block of 128 rows (0 to 127, 128 to 255, ...) at most 48 rows name the same one
- route_weights: float32 [2048, 2], P('dp'), may hold values from 0.1 to 1
- gate_weight: bfloat16 [8, 6144, 8192], P('expert', 'blk', 'dp'), may hold values from -0.078125 to 0.078125
- up_weight: bfloat16 [8, 6144, 8192], P('expert', 'blk', 'dp'), may hold values from -0.078125 to 0.078125
- down_weight: bfloat16 [8, 8192, 6144], P('expert', 'dp', 'blk'), may hold values from -0.0625 to 0.0625
Outputs:
- mixed: bfloat16 [2048, 6144], P('dp', 'blk')
Inputs may be any that keep to these rules, and one draw needn't show every extreme that they name: `expert_ids`: each row names 2 different experts. Among the 128 rows of one data shard no expert is named more than 48 times, and in every draw some expert is named exactly 48 times in some shard.
All inputs are finite; a program needn't handle non-finite values.
Results may differ from a plain program's by a relative error of at most 0.0051.
Values may be sent and summed in bfloat16 or wider, within the bound.
A program may use at most 64 MiB of HBM per device.

v0:
```python
import jax
import jax.numpy as jnp
from jax import lax
from jax.sharding import PartitionSpec as P

EXPERTS = 8
CAP = 48


def local(tokens, expert_ids, route_weights, gate_weight, up_weight, down_weight):
    local_count = gate_weight.shape[0]
    token_count = tokens.shape[0]
    top_count = expert_ids.shape[1]
    group_index = lax.axis_index("expert")
    flat_ids = expert_ids.reshape(-1)
    one_hot = (flat_ids[:, None] == jnp.arange(EXPERTS, dtype=jnp.int32)[None, :]).astype(jnp.int32)
    before = jnp.cumsum(one_hot, axis=0) - one_hot
    position = jnp.sum(before * one_hot, axis=1)
    local_ids = flat_ids - group_index * local_count
    is_mine = local_ids[:, None] == jnp.arange(local_count, dtype=jnp.int32)[None, :]
    in_slot = position[:, None] == jnp.arange(CAP, dtype=jnp.int32)[None, :]
    slot_hit = (is_mine[:, :, None] & in_slot[:, None, :]).reshape(
        token_count, top_count, local_count, CAP
    )
    dispatch = jnp.any(slot_hit, axis=1).astype(jnp.bfloat16)
    combine = jnp.sum(slot_hit.astype(jnp.float32) * route_weights[:, :, None, None], axis=1)
    picked = jnp.einsum("tec,tf->ecf", dispatch, tokens, preferred_element_type=jnp.float32).astype(
        jnp.bfloat16
    )
    shard_rows = lax.all_gather(picked, "dp", axis=1, tiled=True)
    gate_part = jnp.einsum(
        "enf,efh->enh", shard_rows, gate_weight, preferred_element_type=jnp.float32
    )
    up_part = jnp.einsum("enf,efh->enh", shard_rows, up_weight, preferred_element_type=jnp.float32)
    partial_value = jnp.stack([gate_part, up_part])
    summed = lax.psum(partial_value, "blk")
    hidden = (jax.nn.silu(summed[0]) * summed[1]).astype(jnp.bfloat16)
    expert_out = lax.psum_scatter(
        jnp.einsum("enh,ehd->ned", hidden, down_weight, preferred_element_type=jnp.float32),
        "dp",
        scatter_dimension=0,
        tiled=True,
    )
    mixed_part = jnp.einsum("tec,ced->td", combine, expert_out, precision=lax.Precision.HIGHEST)
    mixed = lax.psum(mixed_part, "expert")
    return mixed.astype(jnp.bfloat16)


def solution(mesh):
    placed = (
        P("dp", "blk"),
        P("dp", None),
        P("dp", None),
        P("expert", "blk", "dp"),
        P("expert", "blk", "dp"),
        P("expert", "dp", "blk"),
    )
    return jax.shard_map(
        local, mesh=mesh, in_specs=placed, out_specs=P("dp", "blk"), check_vma=False
    )
```

profile of v0, /device:TPU:2, one launch (start us, length us, event | category | flops | bytes accessed | tf_op | source)
XLA Modules:
  0.0 316.2 jit_solution(18314517861227424447)
XLA Ops:
  6.5 0.0 copy-start
  6.5 0.0 all-gather.2.cloned.1.call-start
  6.5 0.9 copy.13
  7.5 0.1 eq.65
  7.6 0.1 reshape.70
  7.8 0.6 reduce-window.6
  8.4 0.2 slice_reduce_fusion
  8.6 0.1 fusion.7
  8.7 0.1 eq.69
  8.9 0.1 copy.15
  9.0 0.7 broadcast_subtract_fusion
  9.7 1.9 convolution_convert_fusion
  11.6 0.0 all-gather.2.cloned.1.call-update
  11.7 0.0 all-reduce.3.cloned.1.call-start
  11.7 45.8 %all-gather.2.cloned.1.call-done = bf16[2,768,1536]{2,1,0:T(8,128)(2,1)} async-done(((bf16[2,48,1536]{2,1,0:T(8,128)(2,1)}), bf16[2,768,1536]{2,1,0:T(8,128)(2,1)}) %all-gather.2.cloned.1.call-update) | async-done | bytes 4718608 | tf_op jit(solution)/shard_map/all_gather | solution.py:30
  57.5 0.0 copy-start.2
  57.5 0.0 copy-start.3
  57.5 5.5 %convolution_bitcast_fusion.2 = f32[1,2,768,512]{3,2,1,0:T(8,128)S(1)} fusion(bf16[2,768,1536]{2,1,0:T(8,128)(2,1)} %all-gather.2.cloned.1.call-done, bf16[2,1536,512]{2,1,0:T(8,128)(2,1)} %param.10), kind=kOutput, calls=%fused_computation.8 | convolution fusion | flops 2415919104 | bytes 11010048 | tf_op jit(solution)/shard_map/enf,efh->enh/dot_general | solution.py:34
  63.0 0.0 copy-done.2
  63.0 0.1 copy-done.3
  63.1 2.6 convolution_bitcast_fusion.3
  65.7 3.4 %pad_maximum_fusion = f32[2,2,768,512]{3,2,1,0:T(8,128)} fusion(f32[1,2,768,512]{3,2,1,0:T(8,128)S(1)} %convolution_bitcast_fusion.2, f32[1,2,768,512]{3,2,1,0:T(8,128)S(1)} %convolution_bitcast_fusion.3), kind=kLoop, calls=%fused_computation | loop fusion | flops 1572864 | bytes 12582912 | tf_op jit(solution)/shard_map/stack | solution.py:35
  69.1 0.0 all-reduce.3.cloned.1.call-update
  69.1 0.0 reduce-scatter.2.cloned.1.call-start
  69.1 129.7 %all-reduce.3.cloned.1.call-done = f32[2,2,768,512]{3,2,1,0:T(8,128)} async-done(((f32[2,2,768,512]{3,2,1,0:T(8,128)}), f32[2,2,768,512]{3,2,1,0:T(8,128)}) %all-reduce.3.cloned.1.call-update) | async-done | bytes 6291472 | tf_op jit(solution)/shard_map/psum | solution.py:36
  198.9 0.0 copy-done
  198.9 8.0 %convolution_bitcast_fusion = f32[768,2,1536]{2,0,1:T(8,128)} fusion(bf16[2,512,1536]{2,1,0:T(8,128)(2,1)S(1)} %copy-done, f32[2,2,768,512]{3,2,1,0:T(8,128)} %all-reduce.3.cloned.1.call-done), kind=kOutput, calls=%fused_computation.1 | convolution fusion | flops 2420637696 | bytes 18874368 | tf_op jit(solution)/shard_map/enh,ehd->ned/dot_general | solution.py:39
  206.9 0.0 reduce-scatter.2.cloned.1.call-update
  206.9 0.7 copy-done.1
  207.6 73.1 %reduce-scatter.2.cloned.1.call-done = f32[48,2,1536]{2,0,1:T(8,128)} async-done(((f32[768,2,1536]{2,0,1:T(8,128)}), f32[48,2,1536]{2,0,1:T(8,128)}) %reduce-scatter.2.cloned.1.call-update) | async-done | bytes 589840 | tf_op jit(solution)/shard_map/reduce_scatter | solution.py:38
  280.7 2.8 convolution_bitcast_fusion.1
  283.5 26.3 %all-reduce.4 = bf16[128,1536]{1,0:T(8,128)(2,1)} all-reduce(f32[128,1536]{1,0:T(8,128)} %convolution_bitcast_fusion.1), channel_id=1, replica_groups=mesh['dp'=16,'expert'=4,'blk'=4] {'expert'}, use_global_device_ids=true, to_apply=%region_7.8 | all-reduce | flops 196608 | bytes 1179648 | tf_op jit(solution)/shard_map/psum | solution.py:45
  (8 shorter events, 0.1 us)
Async XLA Ops:
  6.5 192.3 %copy-start = (bf16[2,512,1536]{2,1,0:T(8,128)(2,1)S(1)}, bf16[2,512,1536]{2,1,0:T(8,128)(2,1)}, u32[]{:S(2)}) copy-start(bf16[2,512,1536]{2,1,0:T(8,128)(2,1)} %param.11) | copy-start | bytes 9437188
  6.5 50.9 %all-gather.2.cloned.1.call-start = ((), (), s32[]{:S(2)}) async-start(), calls=%async_computation.1 | async-start | bytes 5013504 | tf_op jit(solution)/shard_map/all_gather | solution.py:30
  11.7 187.2 %all-reduce.3.cloned.1.call-start = ((), (), s32[]{:S(2)}) async-start(), calls=%async_computation.2 | async-start | bytes 12582912 | tf_op jit(solution)/shard_map/psum | solution.py:36
  57.5 5.6 %copy-start.2 = (bf16[2,768,1536]{2,1,0:T(8,128)(2,1)S(1)}, bf16[2,768,1536]{2,1,0:T(8,128)(2,1)}, u32[]{:S(2)}) copy-start(bf16[2,768,1536]{2,1,0:T(8,128)(2,1)} %all-gather.2.cloned.1.call-done) | copy-start | bytes 14155780
  57.5 5.6 %copy-start.3 = (bf16[2,1536,512]{2,1,0:T(8,128)(2,1)S(1)}, bf16[2,1536,512]{2,1,0:T(8,128)(2,1)}, u32[]{:S(2)}) copy-start(bf16[2,1536,512]{2,1,0:T(8,128)(2,1)} %param.9) | copy-start | bytes 9437188
  69.1 211.6 %reduce-scatter.2.cloned.1.call-start = ((), (), s32[]{:S(2)}) async-start(), calls=%async_computation.3 | async-start | bytes 10027008 | tf_op jit(solution)/shard_map/reduce_scatter | solution.py:38
  206.9 0.7 copy-start.1
Sparse Core Ops, SparseCore 0:
  11.8 45.6 all-gather.1
  69.2 129.6 all-reduce.2
  207.0 73.5 reduce-scatter.1
where the time goes:
time: 316 us
  waiting for transfers between devices  249 us (79%)
  blocking collectives  26.3 us (8%)
  matrix products  20.9 us (7%)
  between operations  13.2 us (4%)
  other arithmetic  4.85 us (2%)
    psum x1, waiting for transfers between devices, local(): summed = lax.psum(partial_value, 'blk')  130 us
    reduce_scatter x1, waiting for transfers between devices, local(): lax.psum_scatter(jnp.einsum('enh,ehd->ned', hidden, down_weight, preferre...  73.1 us
    all_gather x1, waiting for transfers between devices, local(): shard_rows = lax.all_gather(picked, 'dp', axis=1, tiled=True)  45.8 us
    psum x1, blocking collectives, local(): mixed = lax.psum(mixed_part, 'expert')  26.3 us
    dot_general x1, matrix products, local(): jnp.einsum('enh,ehd->ned', hidden, down_weight, preferred_element_type=jn...  8.03 us
  transfers between devices with their start and end apart: 3, of which 3 were waited for; matrix products, arithmetic and copies ran while one was open for 0% of the time, Pallas kernels for 0%

commit v1 on v0

--- a/solution.py
+++ b/solution.py
@@ -33,7 +33,24 @@
     )
     up_part = jnp.einsum("enf,efh->enh", shard_rows, up_weight, preferred_element_type=jnp.float32)
     partial_value = jnp.stack([gate_part, up_part])
-    summed = lax.psum(partial_value, "blk")
+
+    def wrap_the_numbers(point):
+        shares = lax.psum(1, "blk")
+
+        def _link_meshes(response, block_out):
+            if block_out >= shares:
+                return response
+            return _link_meshes(
+                response
+                + lax.ppermute(
+                    response, axis_name="blk", perm=[(j, j ^ block_out) for j in range(shares)]
+                ),
+                2 * block_out,
+            )
+
+        return _link_meshes(point, 1)
+
+    summed = wrap_the_numbers(partial_value)
     hidden = (jax.nn.silu(summed[0]) * summed[1]).astype(jnp.bfloat16)
     expert_out = lax.psum_scatter(
         jnp.einsum("enh,ehd->ned", hidden, down_weight, preferred_element_type=jnp.float32),

time: 316 us -> 474 us (1.50)
  waiting for transfers between devices: 249 us -> 390 us
  other arithmetic: 4.85 us -> 17.5 us
    ppermute x0 -> x2, waiting for transfers between devices: none -> 274 us  [_link_meshes(): lax.ppermute(response, axis_name='blk', perm=[(j, j ^ block_out) for j in...]
    psum x1 -> x0, waiting for transfers between devices: 130 us -> none  [local(): summed = lax.psum(partial_value, 'blk')]
    add x0 -> x2, other arithmetic: none -> 15 us  [_link_meshes(): response + lax.ppermute(response, axis_name='blk', perm=[(j, j ^ block_ou...]
  transfers between devices with their start and end apart: 3 -> 4, of which waited for: 3 -> 4; matrix products, arithmetic and copies ran while one was open for 0% -> 0% of each run, Pallas kernels for 0% -> 0%
where the time goes in v1:
time: 474 us
  waiting for transfers between devices  390 us (82%)
  blocking collectives  26.5 us (6%)
  matrix products  20.9 us (4%)
  other arithmetic  17.5 us (4%)
  between operations  13.5 us (3%)
    ppermute x2, waiting for transfers between devices, _link_meshes(): lax.ppermute(response, axis_name='blk', perm=[(j, j ^ block_out) for j in...  274 us
    reduce_scatter x1, waiting for transfers between devices, local(): lax.psum_scatter(jnp.einsum('enh,ehd->ned', hidden, down_weight, preferre...  70.7 us
    all_gather x1, waiting for transfers between devices, local(): shard_rows = lax.all_gather(picked, 'dp', axis=1, tiled=True)  45.8 us
    psum x1, blocking collectives, local(): mixed = lax.psum(mixed_part, 'expert')  26.5 us
    add x2, other arithmetic, _link_meshes(): response + lax.ppermute(response, axis_name='blk', perm=[(j, j ^ block_ou...  15 us
  transfers between devices with their start and end apart: 4, of which 4 were waited for; matrix products, arithmetic and copies ran while one was open for 0% of the time, Pallas kernels for 0%

profile of v1, /device:TPU:2, one launch (start us, length us, event | category | flops | bytes accessed | tf_op | source)
XLA Modules:
  0.0 473.7 jit_solution(515828243712616681)
XLA Ops:
  6.5 0.0 copy-start
  6.5 0.0 all-gather.2.cloned.1.call-start
  6.5 0.9 copy.13
  7.5 0.1 eq.65
  7.6 0.1 reshape.70
  7.8 0.6 reduce-window.6
  8.4 0.2 slice_reduce_fusion
  8.6 0.1 fusion.7
  8.7 0.1 eq.69
  8.9 0.1 copy.15
  9.0 0.7 broadcast_subtract_fusion
  9.7 1.9 convolution_convert_fusion
  11.6 0.0 all-gather.2.cloned.1.call-update
  11.7 0.0 reduce-scatter.2.cloned.1.call-start
  11.7 45.8 %all-gather.2.cloned.1.call-done = bf16[2,768,1536]{2,1,0:T(8,128)(2,1)} async-done(((bf16[2,48,1536]{2,1,0:T(8,128)(2,1)}), bf16[2,768,1536]{2,1,0:T(8,128)(2,1)}) %all-gather.2.cloned.1.call-update) | async-done | bytes 4718608 | tf_op jit(solution)/shard_map/all_gather | solution.py:30
  57.5 5.5 %convolution_bitcast_fusion.2 = f32[1,2,768,512]{3,2,1,0:T(8,128)S(1)} fusion(bf16[2,768,1536]{2,1,0:T(8,128)(2,1)} %all-gather.2.cloned.1.call-done, bf16[2,1536,512]{2,1,0:T(8,128)(2,1)} %param.10), kind=kOutput, calls=%fused_computation.8 | convolution fusion | flops 2415919104 | bytes 11010048 | tf_op jit(solution)/shard_map/enf,efh->enh/dot_general | solution.py:34
  63.0 0.0 copy-done.4
  63.0 0.1 copy-done.5
  63.1 2.6 convolution_bitcast_fusion.3
  65.7 1.0 pad_maximum_fusion
  66.7 0.7 collective-permute-start
  67.5 137.0 %collective-permute-done = f32[2,2,768,512]{3,2,1,0:T(8,128)S(1)} collective-permute-done((f32[2,2,768,512]{3,2,1,0:T(8,128)S(1)}, f32[2,2,768,512]{3,2,1,0:T(8,128)S(1)}, u32[]{:S(2)}, u32[]{:S(2)}) %collective-permute-start) | collective-permute-done | bytes 6291488 | tf_op jit(solution)/shard_map/ppermute | solution.py:45
  204.5 4.5 fusion.10
  209.0 2.1 collective-permute-start.1
  211.1 136.6 %collective-permute-done.1 = f32[2,2,768,512]{3,2,1,0:T(8,128)} collective-permute-done((f32[2,2,768,512]{3,2,1,0:T(8,128)}, f32[2,2,768,512]{3,2,1,0:T(8,128)}, u32[]{:S(2)}, u32[]{:S(2)}) %collective-permute-start.1) | collective-permute-done | bytes 6291488 | tf_op jit(solution)/shard_map/ppermute | solution.py:45
  347.7 10.5 %fusion.19 = f32[2,2,768,512]{3,2,1,0:T(8,128)} fusion(f32[2,2,768,512]{3,2,1,0:T(8,128)} %collective-permute-done.1, f32[2,2,768,512]{3,2,1,0:T(8,128)} %copy-done.2, f32[1,2,768,512]{3,2,1,0:T(8,128)S(1)} %convolution_bitcast_fusion.2, f32[1,2,768,512]{3,2,1,0:T(8,128)} %copy-done.1), kind=kLoop, calls=%fused_computation.27 | loop fusion | flops 4718592 | bytes 25165824 | tf_op jit(solution)/shard_map/add | solution.py:44
  358.2 8.0 %convolution_bitcast_fusion = f32[768,2,1536]{2,0,1:T(8,128)} fusion(bf16[2,512,1536]{2,1,0:T(8,128)(2,1)S(1)} %copy-done, f32[2,2,768,512]{3,2,1,0:T(8,128)} %fusion.19), kind=kOutput, calls=%fused_computation.1 | convolution fusion | flops 2420637696 | bytes 18874368 | tf_op jit(solution)/shard_map/enh,ehd->ned/dot_general | solution.py:56
  366.2 0.0 reduce-scatter.2.cloned.1.call-update
  366.2 0.7 copy-done.3
  366.9 70.7 %reduce-scatter.2.cloned.1.call-done = f32[48,2,1536]{2,0,1:T(8,128)} async-done(((f32[768,2,1536]{2,0,1:T(8,128)}), f32[48,2,1536]{2,0,1:T(8,128)}) %reduce-scatter.2.cloned.1.call-update) | async-done | bytes 589840 | tf_op jit(solution)/shard_map/reduce_scatter | solution.py:55
  437.6 2.8 convolution_bitcast_fusion.1
  440.4 26.5 %all-reduce.1 = bf16[128,1536]{1,0:T(8,128)(2,1)} all-reduce(f32[128,1536]{1,0:T(8,128)} %convolution_bitcast_fusion.1), channel_id=1, replica_groups=mesh['dp'=16,'expert'=4,'blk'=4] {'expert'}, use_global_device_ids=true, to_apply=%region_6.7 | all-reduce | flops 196608 | bytes 1179648 | tf_op jit(solution)/shard_map/psum | solution.py:62
  (15 shorter events, 0.1 us)
Async XLA Ops:
  6.5 351.6 %copy-start = (bf16[2,512,1536]{2,1,0:T(8,128)(2,1)S(1)}, bf16[2,512,1536]{2,1,0:T(8,128)(2,1)}, u32[]{:S(2)}) copy-start(bf16[2,512,1536]{2,1,0:T(8,128)(2,1)} %param.11) | copy-start | bytes 9437188
  6.5 50.9 %all-gather.2.cloned.1.call-start = ((), (), s32[]{:S(2)}) async-start(), calls=%async_computation.1 | async-start | bytes 5013504 | tf_op jit(solution)/shard_map/all_gather | solution.py:30
  11.7 425.9 %reduce-scatter.2.cloned.1.call-start = ((), (), s32[]{:S(2)}) async-start(), calls=%async_computation.2 | async-start | bytes 10027008 | tf_op jit(solution)/shard_map/reduce_scatter | solution.py:55
  57.5 5.6 %copy-start.4 = (bf16[2,768,1536]{2,1,0:T(8,128)(2,1)S(1)}, bf16[2,768,1536]{2,1,0:T(8,128)(2,1)}, u32[]{:S(2)}) copy-start(bf16[2,768,1536]{2,1,0:T(8,128)(2,1)} %all-gather.2.cloned.1.call-done) | copy-start | bytes 14155780
  57.5 5.6 %copy-start.5 = (bf16[2,1536,512]{2,1,0:T(8,128)(2,1)S(1)}, bf16[2,1536,512]{2,1,0:T(8,128)(2,1)}, u32[]{:S(2)}) copy-start(bf16[2,1536,512]{2,1,0:T(8,128)(2,1)} %param.9) | copy-start | bytes 9437188
  65.7 138.8 %copy-start.1 = (f32[1,2,768,512]{3,2,1,0:T(8,128)}, f32[1,2,768,512]{3,2,1,0:T(8,128)S(1)}, u32[]{:S(2)}) copy-start(f32[1,2,768,512]{3,2,1,0:T(8,128)S(1)} %convolution_bitcast_fusion.3) | copy-start | bytes 9437188
  66.7 137.8 %collective-permute-start = (f32[2,2,768,512]{3,2,1,0:T(8,128)S(1)}, f32[2,2,768,512]{3,2,1,0:T(8,128)S(1)}, u32[]{:S(2)}, u32[]{:S(2)}) collective-permute-start(f32[2,2,768,512]{3,2,1,0:T(8,128)S(1)} %pad_maximum_fusion), channel_id=1, source_target_pairs={{0,1},{1,0},{2,3},{3,2},{4,5},{5,4},{6,7},{7,6},{8,9},{9,8},{10,11... | collective-permute-start | bytes 18874376 | tf_op jit(solution)/shard_map/ppermute | solution.py:45
  204.5 4.5 copy-start.2
  209.0 138.7 %collective-permute-start.1 = (f32[2,2,768,512]{3,2,1,0:T(8,128)}, f32[2,2,768,512]{3,2,1,0:T(8,128)}, u32[]{:S(2)}, u32[]{:S(2)}) collective-permute-start(f32[2,2,768,512]{3,2,1,0:T(8,128)} %fusion.10), channel_id=1, source_target_pairs={{0,2},{1,3},{2,0},{3,1},{4,6},{5,7},{6,4},{7,5},{8,10},{9,11},{10,... | collective-permute-start | bytes 18874376 | tf_op jit(solution)/shard_map/ppermute | solution.py:45
  366.2 0.7 copy-start.3
Sparse Core Ops, SparseCore 0:
  11.8 45.6 all-gather.1
  366.3 71.2 reduce-scatter.1
